TPU v7x, 32 devices: a whole 2x2x4 slice. The times are simulated.
32 devices in a mesh: groups: 2 (over y), tiles: 4 (over z), rep: 4 (over x, core).
Axes of the slice: x: 2, y: 2, z: 4, core: 2. Of those that a mesh axis runs over, the one named last changes fastest.
Arguments:
- tiles: float32 [512, 256, 256], P(('groups', 'tiles', 'rep')), parts along dimension 0, may hold values from 0 to 1, as said below
- tile_row: int32 [512], P(('groups', 'tiles', 'rep')), parts along dimension 0, may hold values from 0 to 15, as said below
- tile_col: int32 [512], P(('groups', 'tiles', 'rep')), parts along dimension 0, may hold values from 0 to 15
- scaling: float32 [8192], P(('groups', 'tiles')), parts along dimension 0, may hold values from 0.3 to 3
Outputs:
- balanced: float32 [8192], P(('groups', 'tiles')), parts along dimension 0
- residual: float32 [8192], P(('groups', 'tiles')), parts along dimension 0
There are 2 independent parts, one for each index of `groups`. A program takes and returns all parts, laid end to end along the dimension named above; each array names one. Nothing has to cross between parts.
Inputs may be any that keep to these rules, and one draw needn't show every extreme that they name: `tile_row`: blocks of index q of tiles are q * 4 to q * 4 + 3. A tile's row block is at most its column block. Outside the blocks of its own index of tiles and the two indices beside it, the tiles of one device name at most 26 blocks of each index, counted with repetition. `tiles`: entries are not negative.
All inputs are finite; a program needn't handle non-finite values.
Results may differ from a plain program's by a relative error of at most 0.0003.
Values sent between devices are 32-bit elements; how exact they have to be, the bound alone decides.
A program may use at most 64 MiB of HBM per device.

v0:
```python
import jax
import jax.numpy as jnp
from jax import lax
from jax.sharding import PartitionSpec as P

ITERS = 2


def tile_products(tiles, row_blocks, col_blocks, offdiag):
    forward = jnp.einsum("kij,kj->ki", tiles, col_blocks, precision=lax.Precision.HIGHEST)
    backward = jnp.einsum("kij,ki->kj", tiles, row_blocks, precision=lax.Precision.HIGHEST)
    return (forward, jnp.where(offdiag[:, None], backward, 0.0))


def inner_sum(left, right):
    return lax.psum(jnp.sum(left * right), "tiles")


def shards(tiles, tile_row, tile_col, scaling):
    width = tiles.shape[1]
    offdiag = tile_row != tile_col

    def apply_map(vector):
        whole = lax.all_gather(vector, "tiles", axis=0, tiled=True).reshape(-1, width)
        forward, backward = tile_products(tiles, whole[tile_row], whole[tile_col], offdiag)
        dense = jnp.zeros_like(whole).at[tile_row].add(forward).at[tile_col].add(backward)
        share = lax.psum_scatter(dense.reshape(-1), "tiles", scatter_dimension=0, tiled=True)
        return lax.psum(share, "rep")

    load = scaling * apply_map(scaling)
    residual = 1.0 - load
    direction = residual
    update = jnp.zeros_like(scaling)
    norm_now = inner_sum(residual, residual)
    for step in range(ITERS):
        image = scaling * apply_map(scaling * direction) + load * direction
        alpha = norm_now / inner_sum(direction, image)
        update = update + alpha * direction
        residual = residual - alpha * image
        norm_next = inner_sum(residual, residual)
        direction = residual + norm_next / norm_now * direction
        norm_now = norm_next
    return (scaling * (1.0 + update), residual)


def solution(mesh):
    placed = (
        P(("groups", "tiles", "rep"), None, None),
        P(("groups", "tiles", "rep")),
        P(("groups", "tiles", "rep")),
        P(("groups", "tiles")),
    )
    return jax.shard_map(
        shards,
        mesh=mesh,
        in_specs=placed,
        out_specs=(P(("groups", "tiles")), P(("groups", "tiles"))),
        check_vma=False,
    )
```

profile of v0, /device:TPU:0, one launch (start us, length us, event | category | flops | bytes accessed | tf_op | source)
XLA Modules:
  0.0 186.5 jit_solution(14720430533203083417)
XLA Ops:
  0.6 1.2 dynamic-slice
  2.5 0.7 compare_select_fusion.1
  3.2 0.7 compare_select_fusion
  3.8 0.7 ne.3
  4.5 14.9 %all_gather.9 = f32[4096]{0:T(1024)S(1)} all-gather(f32[1024]{0:T(1024)} %param.7), channel_id=1, replica_groups=mesh['groups'=2,'tiles'=4,'rep'=4] {'tiles'}, dimensions={0}, use_global_device_ids=true | all-gather | bytes 20480 | tf_op jit(solution)/shard_map/all_gather | solution.py:24
  20.7 5.7 %fusion.25 = f32[16,1,256]{2,1,0:T(1,128)S(1)} fusion(f32[16,256,256]{2,1,0:T(8,128)} %param.4, f32[16,256,1]{1,0,2:T(8,128)S(1)} %bitcast.41), kind=kOutput, calls=%fused_computation.40 | convolution fusion | flops 12582912 | bytes 4227072 | tf_op jit(solution)/shard_map/kij,kj->ki/dot_general | solution.py:10
  26.3 0.7 scatter_custom_fusion
  27.0 4.3 %fusion.22 = f32[16,1,256]{2,1,0:T(1,128)S(1)} fusion(f32[16,256,256]{2,1,0:T(8,128)} %param.4, f32[16,256,1]{1,0,2:T(8,128)S(1)} %bitcast.38), kind=kOutput, calls=%fused_computation.37 | convolution fusion | flops 12582912 | bytes 4227072 | tf_op jit(solution)/shard_map/kij,ki->kj/dot_general | solution.py:11
  31.3 0.7 scatter_custom_fusion.1
  32.1 18.8 %all-reduce = f32[4096]{0:T(1024)S(1)} all-reduce(f32[4096]{0:T(1024)S(1)} %bitcast.46), channel_id=2, replica_groups=mesh['groups'=2,'tiles'=4,'rep'=4] {'tiles'}, use_global_device_ids=true, to_apply=%region_2.3.clone | all-reduce | flops 4096 | bytes 32768
  50.8 5.6 %psum.49 = f32[1024]{0:T(1024)S(1)} all-reduce(f32[1024]{0:T(1024)S(1)} %dynamic-slice.1), channel_id=1, replica_groups=mesh['groups'=2,'tiles'=4,'rep'=4] {'rep'}, use_global_device_ids=true, to_apply=%region_3.4 | all-reduce | flops 1024 | bytes 8192 | tf_op jit(solution)/shard_map/psum | solution.py:28
  56.5 13.1 %all_gather.10 = f32[4096]{0:T(1024)S(1)} all-gather(f32[1024]{0:T(1024)S(1)} %get-tuple-element.6), channel_id=1, replica_groups=mesh['groups'=2,'tiles'=4,'rep'=4] {'tiles'}, dimensions={0}, use_global_device_ids=true | all-gather | bytes 20480 | tf_op jit(solution)/shard_map/all_gather | solution.py:24
  70.8 5.7 %fusion.19 = f32[16,1,256]{2,1,0:T(1,128)S(1)} fusion(f32[16,256,256]{2,1,0:T(8,128)} %param.4, f32[16,256,1]{1,0,2:T(8,128)S(1)} %bitcast.42), kind=kOutput, calls=%fused_computation.34 | convolution fusion | flops 12582912 | bytes 4227072 | tf_op jit(solution)/shard_map/kij,kj->ki/dot_general | solution.py:10
  76.4 0.7 scatter_custom_fusion.2
  77.1 4.3 %fusion.16 = f32[16,1,256]{2,1,0:T(1,128)S(1)} fusion(f32[16,256,256]{2,1,0:T(8,128)} %param.4, f32[16,256,1]{1,0,2:T(8,128)S(1)} %bitcast.39), kind=kOutput, calls=%fused_computation.31 | convolution fusion | flops 12582912 | bytes 4227072 | tf_op jit(solution)/shard_map/kij,ki->kj/dot_general | solution.py:11
  81.4 0.7 scatter_custom_fusion.3
  82.2 15.5 %all-reduce.1 = f32[4096]{0:T(1024)S(1)} all-reduce(f32[4096]{0:T(1024)S(1)} %bitcast.47), channel_id=3, replica_groups=mesh['groups'=2,'tiles'=4,'rep'=4] {'tiles'}, use_global_device_ids=true, to_apply=%region_8.9.clone | all-reduce | flops 4096 | bytes 32768
  97.7 5.6 %psum.51 = f32[1024]{0:T(1024)S(1)} all-reduce(f32[1024]{0:T(1024)S(1)} %dynamic-slice.3), channel_id=1, replica_groups=mesh['groups'=2,'tiles'=4,'rep'=4] {'rep'}, use_global_device_ids=true, to_apply=%region_9.10 | all-reduce | flops 1024 | bytes 8192 | tf_op jit(solution)/shard_map/psum | solution.py:28
  103.4 0.6 fusion.38
  104.0 9.9 %all-reduce.3 = (f32[]{:T(128)}, f32[]{:T(128)}) all-reduce(f32[]{:T(128)} %get-tuple-element.3, f32[]{:T(128)} %get-tuple-element.2), channel_id=1, replica_groups=mesh['groups'=2,'tiles'=4,'rep'=4] {'tiles'}, use_global_device_ids=true, to_apply=%region_5.6 | all-reduce | flops 2 | bytes 16 | tf_op jit(solution)/shard_map/psum | solution.py:16
  115.2 0.6 multiply_reduce_fusion.1
  115.8 10.1 %psum.53 = f32[]{:T(128)} all-reduce(f32[]{:T(128)} %multiply_reduce_fusion.1), channel_id=1, replica_groups=mesh['groups'=2,'tiles'=4,'rep'=4] {'tiles'}, use_global_device_ids=true, to_apply=%region_13.14 | all-reduce | flops 1 | bytes 8 | tf_op jit(solution)/shard_map/psum | solution.py:16
  127.2 13.1 %all_gather.11 = f32[4096]{0:T(1024)S(1)} all-gather(f32[1024]{0:T(1024)S(1)} %fusion.43), channel_id=1, replica_groups=mesh['groups'=2,'tiles'=4,'rep'=4] {'tiles'}, dimensions={0}, use_global_device_ids=true | all-gather | bytes 20480 | tf_op jit(solution)/shard_map/all_gather | solution.py:24
  141.5 5.7 %fusion.13 = f32[16,1,256]{2,1,0:T(1,128)S(1)} fusion(f32[16,256,256]{2,1,0:T(8,128)} %param.4, f32[16,256,1]{1,0,2:T(8,128)S(1)} %bitcast.40), kind=kOutput, calls=%fused_computation.28 | convolution fusion | flops 12582912 | bytes 4227072 | tf_op jit(solution)/shard_map/kij,kj->ki/dot_general | solution.py:10
  147.2 0.7 scatter_custom_fusion.4
  147.9 4.3 %fusion.10 = f32[16,1,256]{2,1,0:T(1,128)S(1)} fusion(f32[16,256,256]{2,1,0:T(8,128)} %param.4, f32[16,256,1]{1,0,2:T(8,128)S(1)} %bitcast.37), kind=kOutput, calls=%fused_computation.25 | convolution fusion | flops 12582912 | bytes 4227072 | tf_op jit(solution)/shard_map/kij,ki->kj/dot_general | solution.py:11
  152.1 0.7 scatter_custom_fusion.5
  152.9 16.3 %all-reduce.2 = f32[4096]{0:T(1024)S(1)} all-reduce(f32[4096]{0:T(1024)S(1)} %bitcast.48), channel_id=4, replica_groups=mesh['groups'=2,'tiles'=4,'rep'=4] {'tiles'}, use_global_device_ids=true, to_apply=%region_16.17.clone | all-reduce | flops 4096 | bytes 32768
  169.2 5.6 %psum.54 = f32[1024]{0:T(1024)S(1)} all-reduce(f32[1024]{0:T(1024)S(1)} %dynamic-slice.5), channel_id=1, replica_groups=mesh['groups'=2,'tiles'=4,'rep'=4] {'rep'}, use_global_device_ids=true, to_apply=%region_17.18 | all-reduce | flops 1024 | bytes 8192 | tf_op jit(solution)/shard_map/psum | solution.py:28
  174.9 0.6 multiply_reduce_fusion
  175.5 9.1 %psum.55 = f32[]{:T(128)} all-reduce(f32[]{:T(128)} %multiply_reduce_fusion), channel_id=1, replica_groups=mesh['groups'=2,'tiles'=4,'rep'=4] {'tiles'}, use_global_device_ids=true, to_apply=%region_19.20 | all-reduce | flops 1 | bytes 8 | tf_op jit(solution)/shard_map/psum | solution.py:16
  185.9 0.6 multiply_subtract_fusion
  (21 shorter events, 3.5 us)
Async XLA Ops:
  20.6 35.8 %copy-start = (f32[1024]{0:T(1024)S(1)}, f32[1024]{0:T(1024)}, u32[]{:S(2)}) copy-start(f32[1024]{0:T(1024)} %param.7) | copy-start | bytes 12292
where the time goes:
time: 187 us
  blocking collectives  138 us (74%)
  matrix products  29.8 us (16%)
  other arithmetic  8.72 us (5%)
  between operations  5.44 us (3%)
  local copies, waits for them, and re-layouts  4.75 us (3%)
    unnamed x3, blocking collectives  50.6 us
    all_gather x3, blocking collectives, apply_map(): lax.all_gather(vector, 'tiles', axis=0, tiled=True).reshape(-1, width)  41.2 us
    psum x3, blocking collectives, inner_sum(): return lax.psum(jnp.sum(left * right), 'tiles')  29.1 us
    dot_general x3, matrix products, tile_products(): jnp.einsum('kij,kj->ki', tiles, col_blocks, precision=lax.Precision.HIGHEST)  17 us
    psum x3, blocking collectives, apply_map(): return lax.psum(share, 'rep')  16.9 us
    dot_general x3, matrix products, tile_products(): jnp.einsum('kij,ki->kj', tiles, row_blocks, precision=lax.Precision.HIGHEST)  12.8 us
    scatter-add x6, other arithmetic, apply_map(): jnp.zeros_like(whole).at[tile_row].add(forward).at[tile_col].add(backward)  4.27 us

commit v1 on v0

v1 whole, which is shorter than its diff:
```python
import functools
import jax
import jax.numpy as jnp
from jax import lax
from jax.experimental import pallas as pl
from jax.experimental.pallas import tpu as pltpu
from jax.sharding import PartitionSpec as P

ITERS = 2
LANES = 128
MESH = pl.DeviceIdType.MESH


def split_exact(x):
    high = x.astype(jnp.bfloat16)
    rest = x - high.astype(jnp.float32)
    mid = rest.astype(jnp.bfloat16)
    low = (rest - mid.astype(jnp.float32)).astype(jnp.bfloat16)
    return jnp.concatenate([high, mid, low], axis=0)


def kernel(sizes, tiles_hbm, row_ref, col_ref, scaling_hbm, balanced_hbm, residual_hbm,
           mats, pick, spread, dense, shares, vectors, result,
           tile_sem, scale_sem, send_sem, recv_sem, out_sem):
    count, blocks, reps, owned, halves = sizes
    places = blocks // owned
    peers = places * reps
    q = lax.axis_index("tiles")
    r = lax.axis_index("rep")
    me = q * reps + r
    rows = blocks * halves
    width = halves * LANES

    def peer_id(offset):
        other = lax.rem(me + offset, peers)
        return other, {"tiles": other // reps, "rep": lax.rem(other, reps)}

    def tile_copy(k):
        return pltpu.make_async_copy(tiles_hbm.at[k], mats.at[count + k], tile_sem.at[k])

    for k in range(count):
        tile_copy(k).start()
    own = pl.ds(q * owned, owned)
    own_scale = pltpu.make_async_copy(scaling_hbm, vectors.at[0, own], scale_sem)
    own_scale.start()

    barrier = pltpu.get_barrier_semaphore()

    @pl.loop(1, peers)
    def _(offset):
        _, target = peer_id(offset)
        pl.semaphore_signal(barrier, inc=1, device_id=target, device_id_type=MESH)

    half_row = lax.broadcasted_iota(jnp.int32, (rows, width), 0)
    half = lax.broadcasted_iota(jnp.int32, (rows, width), 1) // LANES

    @pl.loop(0, count)
    def _(k):
        row, col = row_ref[k], col_ref[k]
        ahead = jnp.where(half_row == halves * col + half, 1.0, 0.0)
        wanted = jnp.where(row != col, halves * row, -halves)
        back = jnp.where(half_row == wanted + half, 1.0, 0.0)
        for part in range(3):
            pick[k, part * rows:(part + 1) * rows, :] = ahead.astype(jnp.bfloat16)
            pick[count + k, part * rows:(part + 1) * rows, :] = back.astype(jnp.bfloat16)

    pl.semaphore_wait(barrier, peers - 1)

    @pl.loop(1, places)
    def _(offset):
        pltpu.make_async_remote_copy(
            src_ref=scaling_hbm, dst_ref=vectors.at[0, own],
            send_sem=send_sem.at[0], recv_sem=recv_sem.at[0],
            device_id={"tiles": lax.rem(q + offset, places)}, device_id_type=MESH,
        ).start()

    @pl.loop(0, count)
    def _(k):
        tile_copy(k).wait()
        mats[k] = mats[count + k].T

    own_scale.wait()
    others = pl.ds(0, (places - 1) * owned)
    pltpu.make_async_copy(vectors.at[0, others], vectors.at[0, others], recv_sem.at[0]).wait()

    def read(slot):
        return vectors[slot].reshape(rows, LANES)

    line = lax.broadcasted_iota(jnp.int32, (rows, LANES), 0)
    rest = pl.ds(0, peers - 1)

    def apply_map(vector, turn):
        parts = split_exact(vector)

        def widen(k, carry):
            wide = lax.dot_general(parts, pick[k], (((0,), (0,)), ((), ())),
                                   preferred_element_type=jnp.float32)
            for h in range(halves):
                spread[k, h * LANES:(h + 1) * LANES, :] = wide[:, h * LANES:(h + 1) * LANES]
            return carry

        lax.fori_loop(0, 2 * count, widen, 0, unroll=8)

        def one(matrix, place, total):
            x = spread[matrix].reshape(-1, 8, LANES)
            for h in range(halves):
                block = mats[matrix, :, h * LANES:(h + 1) * LANES].reshape(-1, 8, LANES)
                product = jnp.sum(jnp.sum(block * x, axis=0), axis=0, keepdims=True)
                total = total + jnp.where(line == halves * place + h, product, 0.0)
            return total

        def both(k, total):
            total = one(k, row_ref[k], total)
            return one(count + k, col_ref[k], total)

        total = lax.fori_loop(0, count, both, jnp.zeros((rows, LANES), jnp.float32), unroll=2)
        dense[turn] = total.reshape(blocks, halves, LANES)
        shares[turn, me] = dense[turn, me]

        @pl.loop(1, peers)
        def _(offset):
            other, target = peer_id(offset)
            pltpu.make_async_remote_copy(
                src_ref=dense.at[turn, other], dst_ref=shares.at[turn, me],
                send_sem=send_sem.at[1 + 2 * turn], recv_sem=recv_sem.at[1 + 2 * turn],
                device_id=target, device_id_type=MESH,
            ).start()

        pltpu.make_async_copy(shares.at[turn, rest], shares.at[turn, rest], recv_sem.at[1 + 2 * turn]).wait()
        vectors[1 + turn, me] = jnp.sum(shares[turn], axis=0)

        @pl.loop(1, peers)
        def _(offset):
            _, target = peer_id(offset)
            pltpu.make_async_remote_copy(
                src_ref=vectors.at[1 + turn, me], dst_ref=vectors.at[1 + turn, me],
                send_sem=send_sem.at[2 + 2 * turn], recv_sem=recv_sem.at[2 + 2 * turn],
                device_id=target, device_id_type=MESH,
            ).start()

        pltpu.make_async_copy(vectors.at[1 + turn, rest], vectors.at[1 + turn, rest], recv_sem.at[2 + 2 * turn]).wait()
        return read(1 + turn)

    def inner(a, b):
        return jnp.sum(a * b, keepdims=True)

    scaling = read(0)
    load = scaling * apply_map(scaling, 0)
    residual = 1.0 - load
    direction = residual
    update = jnp.zeros_like(load)
    norm_now = inner(residual, residual)
    for step in range(ITERS):
        image = scaling * apply_map(scaling * direction, 1 + step) + load * direction
        alpha = norm_now / inner(direction, image)
        update = update + alpha * direction
        residual = residual - alpha * image
        if step + 1 < ITERS:
            norm_next = inner(residual, residual)
            direction = residual + (norm_next / norm_now) * direction
            norm_now = norm_next
    result[0] = (scaling * (1.0 + update)).reshape(blocks, halves, LANES)
    result[1] = residual.reshape(blocks, halves, LANES)
    outs = [pltpu.make_async_copy(result.at[i, own], ref, out_sem.at[i])
            for i, ref in enumerate((balanced_hbm, residual_hbm))]
    for out in outs:
        out.start()
    pltpu.make_async_copy(vectors.at[0, others], vectors.at[0, others], send_sem.at[0]).wait()
    for turn in range(1 + ITERS):
        for phase in range(2):
            pltpu.make_async_copy(shares.at[turn, rest], shares.at[turn, rest],
                                  send_sem.at[1 + 2 * turn + phase]).wait()
    for out in outs:
        out.wait()


def shards(places, reps, tiles, tile_row, tile_col, scaling):
    count, width, _ = tiles.shape
    halves = width // LANES
    owned = scaling.shape[0] // width
    blocks = owned * places
    assert owned == reps
    rows = blocks * halves
    turns = 1 + ITERS
    any_space = pl.BlockSpec(memory_space=pl.ANY)
    smem = pl.BlockSpec(memory_space=pltpu.SMEM)
    shape = jax.ShapeDtypeStruct((owned, halves, LANES), jnp.float32)
    balanced, residual = pl.pallas_call(
        functools.partial(kernel, (count, blocks, reps, owned, halves)),
        out_shape=(shape, shape),
        in_specs=[any_space, smem, smem, any_space],
        out_specs=(any_space, any_space),
        scratch_shapes=[
            pltpu.VMEM((2 * count, width, width), jnp.float32),
            pltpu.VMEM((2 * count, 3 * rows, width), jnp.bfloat16),
            pltpu.VMEM((2 * count, width, LANES), jnp.float32),
            pltpu.VMEM((turns, blocks, halves, LANES), jnp.float32),
            pltpu.VMEM((turns, blocks, halves, LANES), jnp.float32),
            pltpu.VMEM((1 + turns, blocks, halves, LANES), jnp.float32),
            pltpu.VMEM((2, blocks, halves, LANES), jnp.float32),
            pltpu.SemaphoreType.DMA((count,)),
            pltpu.SemaphoreType.DMA,
            pltpu.SemaphoreType.DMA((1 + 2 * turns,)),
            pltpu.SemaphoreType.DMA((1 + 2 * turns,)),
            pltpu.SemaphoreType.DMA((2,)),
        ],
        compiler_params=pltpu.CompilerParams(
            collective_id=0, has_side_effects=True, vmem_limit_bytes=52 * 2**20),
    )(tiles, tile_row, tile_col, scaling.reshape(owned, halves, LANES))
    return balanced.reshape(-1), residual.reshape(-1)


def solution(mesh):
    placed = (
        P(("groups", "tiles", "rep"), None, None),
        P(("groups", "tiles", "rep")),
        P(("groups", "tiles", "rep")),
        P(("groups", "tiles")),
    )
    return jax.shard_map(
        functools.partial(shards, mesh.shape["tiles"], mesh.shape["rep"]),
        mesh=mesh,
        in_specs=placed,
        out_specs=(P(("groups", "tiles")), P(("groups", "tiles"))),
        check_vma=False,
    )
```

time: 187 us -> 44.9 us (0.24)
  blocking collectives: 138 us -> 0 us
  Pallas kernels: 0 us -> 40.9 us
  matrix products: 29.8 us -> 0 us
  other arithmetic: 8.72 us -> 0 us
  between operations: 5.44 us -> 0.65 us
    unnamed x3 -> x0, blocking collectives: 50.6 us -> none
    psum x6 -> x0, blocking collectives: 46 us -> none  [the longest x3 29.1 us: inner_sum(): return lax.psum(jnp.sum(left * right), 'tiles')]
    all_gather x3 -> x0, blocking collectives: 41.2 us -> none  [apply_map(): lax.all_gather(vector, 'tiles', axis=0, tiled=True).reshape(-1, width)]
    pallas_call x0 -> x1, Pallas kernels: none -> 40.9 us  [shards(): pl.pallas_call(functools.partial(kernel, (count, blocks, reps, owned, hal...]
    dot_general x6 -> x0, matrix products: 29.8 us -> none  [the longest x3 17 us: tile_products(): jnp.einsum('kij,kj->ki', tiles, col_blocks, precision=lax.Precision.HIGHEST)]
    scatter-add x6 -> x0, other arithmetic: 4.27 us -> none  [apply_map(): jnp.zeros_like(whole).at[tile_row].add(forward).at[tile_col].add(backward)]
    gather x6 -> x0, local copies, waits for them, and re-layouts: 3.45 us -> none  [the longest x3 1.73 us: apply_map(): whole[tile_col]]
    unnamed x9 -> x8, local copies, waits for them, and re-layouts: 1.28 us -> 3.18 us
where the time goes in v1:
time: 44.9 us; the launch traced here: 44.7 us
  Pallas kernels  40.9 us (91%)
  local copies, waits for them, and re-layouts  3.18 us (7%)
  between operations  0.65 us (1%)
    pallas_call x1, Pallas kernels, shards(): pl.pallas_call(functools.partial(kernel, (count, blocks, reps, owned, hal...  40.9 us
    unnamed x8, local copies, waits for them, and re-layouts  3.18 us

profile of v1, /device:TPU:0, one launch (start us, length us, event | category | flops | bytes accessed | tf_op | source)
XLA Modules:
  0.0 44.7 jit_solution(12764674212385698948)
XLA Ops:
  0.6 0.0 copy-start
  0.6 0.7 %copy-done = f32[1024]{0:T(1024)S(1)} copy-done((f32[1024]{0:T(1024)S(1)}, f32[1024]{0:T(1024)}, u32[]{:S(2)}) %copy-start) | copy-done | bytes 4120
  1.3 0.0 copy-start.1
  1.3 0.7 %copy-done.1 = s32[16]{0:T(128)S(1)} copy-done((s32[16]{0:T(128)S(1)}, s32[16]{0:T(128)}, u32[]{:S(2)}) %copy-start.1) | copy-done | bytes 88
  2.0 0.0 copy-start.2
  2.0 0.7 %copy-done.2 = s32[16]{0:T(128)S(1)} copy-done((s32[16]{0:T(128)S(1)}, s32[16]{0:T(128)}, u32[]{:S(2)}) %copy-start.2) | copy-done | bytes 88
  2.6 40.9 %shard_map.59 = (f32[4,2,128]{2,1,0:T(2,128)S(1)}, f32[4,2,128]{2,1,0:T(2,128)S(1)}) custom-call(f32[16,256,256]{2,1,0:T(8,128)} %tiles_hbm.1, s32[16]{0:T(128)S(1)} %copy-done.1, s32[16]{0:T(128)S(1)} %copy-done.2, f32[4,2,128]{2,1,0:T(2,128)S(1)} %bitcast.5), custom_call_target="tpu_custom_call" | custom-call | tf_op jit(solution)/shard_map/pallas_call | solution.py:188
  43.5 0.6 %copy.8 = f32[1024]{0:T(1024)} copy(f32[1024]{0:T(1024)S(1)} %bitcast.4) | data formatting | bytes 8192
  44.1 0.6 %copy.9 = f32[1024]{0:T(1024)} copy(f32[1024]{0:T(1024)S(1)} %bitcast.3) | data formatting | bytes 8192
Async XLA Ops:
  0.6 0.7 %copy-start = (f32[1024]{0:T(1024)S(1)}, f32[1024]{0:T(1024)}, u32[]{:S(2)}) copy-start(f32[1024]{0:T(1024)} %param.7) | copy-start | bytes 12292
  1.3 0.7 %copy-start.1 = (s32[16]{0:T(128)S(1)}, s32[16]{0:T(128)}, u32[]{:S(2)}) copy-start(s32[16]{0:T(128)} %row_ref.1) | copy-start | bytes 196
  2.0 0.7 %copy-start.2 = (s32[16]{0:T(128)S(1)}, s32[16]{0:T(128)}, u32[]{:S(2)}) copy-start(s32[16]{0:T(128)} %col_ref.1) | copy-start | bytes 196

commit v2 on v0

v2 whole, which is shorter than its diff:
```python
import functools
import jax
import jax.numpy as jnp
from jax import lax
from jax.experimental import pallas as pl
from jax.experimental.pallas import tpu as pltpu
from jax.sharding import PartitionSpec as P

ITERS = 2
LANES = 128
MESH = pl.DeviceIdType.MESH


def split_exact(x):
    high = x.astype(jnp.bfloat16)
    rest = x - high.astype(jnp.float32)
    mid = rest.astype(jnp.bfloat16)
    low = (rest - mid.astype(jnp.float32)).astype(jnp.bfloat16)
    return jnp.concatenate([high, mid, low], axis=0)


def wrap(index, size):
    return jnp.where(index >= size, index - size, index)


def kernel(sizes, tiles_hbm, row_ref, col_ref, scaling_ref, balanced_ref, residual_ref,
           mats, pick, spread, dense, mate, shares, vectors, state, ends, dots,
           tile_sem, scale_sem, send_sem, recv_sem, mate_send, mate_recv, dot_send, dot_recv):
    count, blocks, reps, owned, halves, paired = sizes
    places = blocks // owned
    q = lax.axis_index("tiles")
    r = lax.axis_index("rep")
    rows = blocks * halves
    width = halves * LANES
    chunk = pick.shape[0]
    lanes = 2 if paired else 1
    turn_reps = reps // lanes
    mine = r // lanes
    side = r - mine * lanes
    me = q * turn_reps + mine
    members = places * turn_reps
    final = ITERS if paired else -1

    def for_peers(act):
        def column(ahead, first):
            place = wrap(q + ahead, places)
            for turn in range(first, turn_reps):
                member = wrap(mine + turn, turn_reps)
                act(place, place * turn_reps + member, {"tiles": place, "rep": member * lanes + side})

        if places <= 8:
            for ahead in range(places - 1, 0, -1):
                column(ahead, 0)
        else:
            pl.loop(1, places)(lambda ahead: column(ahead, 0))
        column(0, 1)

    partner = {"rep": r + 1 - 2 * side}

    def tile_copy(k):
        return pltpu.make_async_copy(tiles_hbm.at[k], mats.at[count + k], tile_sem.at[k])

    barrier = pltpu.get_barrier_semaphore()

    @for_peers
    def _(place, member, target):
        pl.semaphore_signal(barrier, inc=1, device_id=target, device_id_type=MESH)

    if paired:
        pl.semaphore_signal(barrier, inc=1, device_id=partner, device_id_type=MESH)

    for k in range(count):
        tile_copy(k).start()
    own = pl.ds(q * owned, owned)
    own_scale = pltpu.make_async_copy(scaling_ref, vectors.at[0, own], scale_sem)
    own_scale.start()

    half_row = lax.broadcasted_iota(jnp.int32, (chunk * halves, width), 0)
    half = lax.broadcasted_iota(jnp.int32, (chunk * halves, width), 1) // LANES

    @pl.loop(0, chunk)
    def _(b):
        hot = jnp.where(half_row == halves * b + half, 1.0, 0.0).astype(jnp.bfloat16)
        pick[b] = jnp.concatenate([hot, hot, hot], axis=0)

    pl.semaphore_wait(barrier, members if paired else members - 1)

    for ahead in range(places - 1, 0, -1):
        pltpu.make_async_remote_copy(
            src_ref=scaling_ref, dst_ref=vectors.at[0, own],
            send_sem=send_sem.at[0], recv_sem=recv_sem.at[0],
            device_id={"tiles": wrap(q + ahead, places)}, device_id_type=MESH,
        ).start()

    @pl.loop(0, count)
    def _(k):
        tile_copy(k).wait()
        mats[k] = mats[count + k].T

    own_scale.wait()
    others = pl.ds(0, (places - 1) * owned)
    rest = pl.ds(0, members - 1)
    pltpu.make_async_copy(vectors.at[0, others], vectors.at[0, others], recv_sem.at[0]).wait()

    line = lax.broadcasted_iota(jnp.int32, (rows, LANES), 0)

    def products(vector):
        for first in range(0, blocks, chunk):
            parts = split_exact(vector[first * halves:(first + chunk) * halves]).T

            def widen(b, carry):
                wide = jnp.dot(parts, pick[b], preferred_element_type=jnp.float32)
                for h in range(halves):
                    spread[first + b, h * LANES:(h + 1) * LANES, :] = wide[:, h * LANES:(h + 1) * LANES]
                return carry

            lax.fori_loop(0, chunk, widen, 0, unroll=True)

        def one(matrix, source, place, total):
            x = spread[source].reshape(-1, 8, LANES)
            for h in range(halves):
                block = mats[matrix, :, h * LANES:(h + 1) * LANES].reshape(-1, 8, LANES)
                product = jnp.sum(jnp.sum(block * x, axis=0), axis=0, keepdims=True)
                total = total + jnp.where(line == halves * place + h, product, 0.0)
            return total

        def both(k, total):
            row, col = row_ref[k], col_ref[k]
            total = one(k, col, row, total)
            return one(count + k, row, jnp.where(row == col, -1, col), total)

        return lax.fori_loop(0, count, both, jnp.zeros((rows, LANES), jnp.float32), unroll=2)

    def with_partner(total, turn):
        dense[turn] = total.reshape(blocks, halves, LANES)
        swap = pltpu.make_async_remote_copy(
            src_ref=dense.at[turn], dst_ref=mate.at[turn],
            send_sem=mate_send.at[turn], recv_sem=mate_recv.at[turn],
            device_id=partner, device_id_type=MESH)
        swap.start()
        swap.wait()
        return total + mate[turn].reshape(rows, LANES)

    def send(source, target_ref, slot, device):
        pltpu.make_async_remote_copy(
            src_ref=source, dst_ref=target_ref, send_sem=send_sem.at[slot],
            recv_sem=recv_sem.at[slot], device_id=device, device_id_type=MESH,
        ).start()

    def take(ref, semaphore):
        pltpu.make_async_copy(ref, ref, semaphore).wait()

    def summed_pairs(vector, turn):
        total = with_partner(products(vector), turn)
        shares[turn, me] = total.reshape(blocks, halves, LANES)

        @for_peers
        def _(place, member, target):
            send(shares.at[turn, me], shares.at[turn, me], 1 + turn, target)

        take(shares.at[turn, rest], recv_sem.at[1 + turn])
        return jnp.sum(shares[turn], axis=0).reshape(rows, LANES)

    def summed_blocks(vector, turn):
        dense[turn] = products(vector).reshape(blocks, halves, LANES)
        shares[turn, me] = dense[turn, me]
        slot = 1 + 2 * turn

        @for_peers
        def _(place, member, target):
            send(dense.at[turn, member], shares.at[turn, me], slot, target)

        take(shares.at[turn, rest], recv_sem.at[slot])
        vectors[1 + turn, me] = jnp.sum(shares[turn], axis=0)

        @for_peers
        def _(place, member, target):
            send(vectors.at[1 + turn, me], vectors.at[1 + turn, me], slot + 1, target)

        take(vectors.at[1 + turn, rest], recv_sem.at[slot + 1])
        return vectors[1 + turn].reshape(rows, LANES)

    apply_map = summed_pairs if paired else summed_blocks

    def inner(a, b):
        return jnp.sum(a * b, keepdims=True)

    scaling = vectors[0].reshape(rows, LANES)
    load = scaling * apply_map(scaling, 0)
    residual = 1.0 - load
    direction = residual
    update = jnp.zeros_like(load)
    norm_now = inner(residual, residual)
    for step in range(ITERS):
        turn = 1 + step
        if turn == final:
            break
        image = scaling * apply_map(scaling * direction, turn) + load * direction
        alpha = norm_now / inner(direction, image)
        update = update + alpha * direction
        residual = residual - alpha * image
        if step + 1 < ITERS:
            norm_next = inner(residual, residual)
            direction = residual + (norm_next / norm_now) * direction
            norm_now = norm_next

    kept = [scaling * (1.0 + update), residual]
    if paired:
        kept += [scaling, load * direction, direction]
    for i, value in enumerate(kept):
        state[i] = value.reshape(blocks, halves, LANES)
    if paired:
        scaled = scaling * direction
        known = inner(load * direction, direction)
        total = with_partner(products(scaled), final)
        dense[1 + final] = total.reshape(blocks, halves, LANES)
        ends[me] = dense[1 + final, own]
        dots[me] = jnp.broadcast_to(inner(scaled, total), (1, LANES))

        @for_peers
        def _(place, member, target):
            send(dense.at[1 + final, pl.ds(place * owned, owned)], ends.at[me], 1 + final, target)
            pltpu.make_async_remote_copy(
                src_ref=dots.at[me], dst_ref=dots.at[me], send_sem=dot_send,
                recv_sem=dot_recv, device_id=target, device_id_type=MESH,
            ).start()

        take(dots.at[rest], dot_recv)
        alpha = norm_now / (known + jnp.sum(dots[...], axis=0)[:, :1])
        take(ends.at[rest], recv_sem.at[1 + final])
        image = state[2, own] * jnp.sum(ends[...], axis=0) + state[3, own]
        balanced_ref[...] = state[0, own] + state[2, own] * (alpha * state[4, own])
        residual_ref[...] = state[1, own] - alpha * image
    else:
        balanced_ref[...] = state[0, own]
        residual_ref[...] = state[1, own]

    take(vectors.at[0, others], send_sem.at[0])
    if paired:
        for turn in range(final):
            take(shares.at[turn, rest], send_sem.at[1 + turn])
        take(ends.at[rest], send_sem.at[1 + final])
        take(dots.at[rest], dot_send)
    else:
        for slot in range(1, 3 + 2 * ITERS):
            take(shares.at[0, rest], send_sem.at[slot])


def shards(places, reps, tiles, tile_row, tile_col, scaling):
    count, width, _ = tiles.shape
    halves = width // LANES
    owned = scaling.shape[0] // width
    blocks = owned * places
    assert owned == reps
    turns = 1 + ITERS
    paired = reps % 2 == 0 and places * reps <= 32
    chunk = 16 if blocks % 16 == 0 else blocks
    members = blocks // 2 if paired else blocks
    block = (halves, LANES)
    any_space = pl.BlockSpec(memory_space=pl.ANY)
    smem = pl.BlockSpec(memory_space=pltpu.SMEM)
    vmem = pl.BlockSpec(memory_space=pltpu.VMEM)
    shape = jax.ShapeDtypeStruct((owned,) + block, jnp.float32)
    slots = 1 + 2 * turns

    def scratch(*dims):
        return pltpu.VMEM(dims + block, jnp.float32)

    balanced, residual = pl.pallas_call(
        functools.partial(kernel, (count, blocks, reps, owned, halves, paired)),
        out_shape=(shape, shape),
        in_specs=[any_space, smem, smem, any_space],
        out_specs=(vmem, vmem),
        scratch_shapes=[
            pltpu.VMEM((2 * count, width, width), jnp.float32),
            pltpu.VMEM((chunk, 3 * chunk * halves, width), jnp.bfloat16),
            pltpu.VMEM((blocks, width, LANES), jnp.float32),
            scratch(turns + 1, blocks),
            scratch(turns, blocks),
            scratch(turns, members, blocks) if paired else scratch(turns, members),
            scratch(1 + turns, blocks),
            scratch(5, blocks),
            scratch(members, owned),
            pltpu.VMEM((members, 1, LANES), jnp.float32),
            pltpu.SemaphoreType.DMA((count,)),
            pltpu.SemaphoreType.DMA,
            pltpu.SemaphoreType.DMA((slots,)),
            pltpu.SemaphoreType.DMA((slots,)),
            pltpu.SemaphoreType.DMA((turns,)),
            pltpu.SemaphoreType.DMA((turns,)),
            pltpu.SemaphoreType.DMA,
            pltpu.SemaphoreType.DMA,
        ],
        compiler_params=pltpu.CompilerParams(
            collective_id=0, has_side_effects=True, vmem_limit_bytes=56 * 2**20),
    )(tiles, tile_row, tile_col, scaling.reshape((owned,) + block))
    return balanced.reshape(-1), residual.reshape(-1)


def solution(mesh):
    placed = (
        P(("groups", "tiles", "rep"), None, None),
        P(("groups", "tiles", "rep")),
        P(("groups", "tiles", "rep")),
        P(("groups", "tiles")),
    )
    return jax.shard_map(
        functools.partial(shards, mesh.shape["tiles"], mesh.shape["rep"]),
        mesh=mesh,
        in_specs=placed,
        out_specs=(P(("groups", "tiles")), P(("groups", "tiles"))),
        check_vma=False,
    )
```

time: 187 us -> 36.4 us (0.19)
  blocking collectives: 138 us -> 0 us
  Pallas kernels: 0 us -> 33 us
  matrix products: 29.8 us -> 0 us
  other arithmetic: 8.72 us -> 0 us
  between operations: 5.44 us -> 0.64 us
  local copies, waits for them, and re-layouts: 4.75 us -> 2.53 us
    unnamed x3 -> x0, blocking collectives: 50.6 us -> none
    psum x6 -> x0, blocking collectives: 46 us -> none  [the longest x3 29.1 us: inner_sum(): return lax.psum(jnp.sum(left * right), 'tiles')]
    all_gather x3 -> x0, blocking collectives: 41.2 us -> none  [apply_map(): lax.all_gather(vector, 'tiles', axis=0, tiled=True).reshape(-1, width)]
    pallas_call x0 -> x1, Pallas kernels: none -> 33 us  [shards(): pl.pallas_call(functools.partial(kernel, (count, blocks, reps, owned, hal...]
    dot_general x6 -> x0, matrix products: 29.8 us -> none  [the longest x3 17 us: tile_products(): jnp.einsum('kij,kj->ki', tiles, col_blocks, precision=lax.Precision.HIGHEST)]
    scatter-add x6 -> x0, other arithmetic: 4.27 us -> none  [apply_map(): jnp.zeros_like(whole).at[tile_row].add(forward).at[tile_col].add(backward)]
    gather x6 -> x0, local copies, waits for them, and re-layouts: 3.45 us -> none  [the longest x3 1.73 us: apply_map(): whole[tile_col]]
where the time goes in v2:
time: 36.4 us; the launch traced here: 36.2 us
  Pallas kernels  33 us (91%)
  local copies, waits for them, and re-layouts  2.53 us (7%)
  between operations  0.64 us (2%)
    pallas_call x1, Pallas kernels, shards(): pl.pallas_call(functools.partial(kernel, (count, blocks, reps, owned, hal...  33 us
    unnamed x2, local copies, waits for them, and re-layouts  2.53 us

profile of v2, /device:TPU:0, one launch (start us, length us, event | category | flops | bytes accessed | tf_op | source)
XLA Modules:
  0.0 36.2 jit_solution(4281996978588403894)
XLA Ops:
  0.6 33.0 %shard_map.59 = (f32[4,2,128]{2,1,0:T(2,128)}, f32[4,2,128]{2,1,0:T(2,128)}) custom-call(f32[16,256,256]{2,1,0:T(8,128)} %tiles_hbm.1, s32[16]{0:T(128)} %row_ref.1, s32[16]{0:T(128)} %col_ref.1, f32[4,2,128]{2,1,0:T(2,128)} %bitcast.5), custom_call_target="tpu_custom_call" | custom-call | tf_op jit(solution)/shard_map/pallas_call | solution.py:269
  33.7 1.3 %copy.8 = f32[1024]{0:T(1024)} copy(f32[1024]{0:T(1024)} %bitcast.4) | data formatting | bytes 8192
  34.9 1.3 %copy.9 = f32[1024]{0:T(1024)} copy(f32[1024]{0:T(1024)} %bitcast.3) | data formatting | bytes 8192

commit v3 on v2

--- a/solution.py
+++ b/solution.py
@@ -23,9 +23,10 @@
     return jnp.where(index >= size, index - size, index)
 
 
-def kernel(sizes, tiles_hbm, row_ref, col_ref, scaling_ref, balanced_ref, residual_ref,
+def kernel(sizes, tiles_hbm, row_hbm, col_hbm, scaling_ref, out_ref,
+           row_ref, col_ref,
            mats, pick, spread, dense, mate, shares, vectors, state, ends, dots,
-           tile_sem, scale_sem, send_sem, recv_sem, mate_send, mate_recv, dot_send, dot_recv):
+           tile_sem, scale_sem, index_sem, send_sem, recv_sem, mate_send, mate_recv, dot_send, dot_recv):
     count, blocks, reps, owned, halves, paired = sizes
     places = blocks // owned
     q = lax.axis_index("tiles")
@@ -69,6 +70,10 @@
     if paired:
         pl.semaphore_signal(barrier, inc=1, device_id=partner, device_id_type=MESH)
 
+    indices = [pltpu.make_async_copy(source, held, index_sem.at[i])
+               for i, (source, held) in enumerate(((row_hbm, row_ref), (col_hbm, col_ref)))]
+    for copy in indices:
+        copy.start()
     for k in range(count):
         tile_copy(k).start()
     own = pl.ds(q * owned, owned)
@@ -83,11 +88,14 @@
         hot = jnp.where(half_row == halves * b + half, 1.0, 0.0).astype(jnp.bfloat16)
         pick[b] = jnp.concatenate([hot, hot, hot], axis=0)
 
+    own_scale.wait()
+    for copy in indices:
+        copy.wait()
     pl.semaphore_wait(barrier, members if paired else members - 1)
 
     for ahead in range(places - 1, 0, -1):
         pltpu.make_async_remote_copy(
-            src_ref=scaling_ref, dst_ref=vectors.at[0, own],
+            src_ref=vectors.at[0, own], dst_ref=vectors.at[0, own],
             send_sem=send_sem.at[0], recv_sem=recv_sem.at[0],
             device_id={"tiles": wrap(q + ahead, places)}, device_id_type=MESH,
         ).start()
@@ -97,7 +105,6 @@
         tile_copy(k).wait()
         mats[k] = mats[count + k].T
 
-    own_scale.wait()
     others = pl.ds(0, (places - 1) * owned)
     rest = pl.ds(0, members - 1)
     pltpu.make_async_copy(vectors.at[0, others], vectors.at[0, others], recv_sem.at[0]).wait()
@@ -129,7 +136,7 @@
             total = one(k, col, row, total)
             return one(count + k, row, jnp.where(row == col, -1, col), total)
 
-        return lax.fori_loop(0, count, both, jnp.zeros((rows, LANES), jnp.float32), unroll=2)
+        return lax.fori_loop(0, count, both, jnp.zeros((rows, LANES), jnp.float32), unroll=8)
 
     def with_partner(total, turn):
         dense[turn] = total.reshape(blocks, halves, LANES)
@@ -229,11 +236,11 @@
         alpha = norm_now / (known + jnp.sum(dots[...], axis=0)[:, :1])
         take(ends.at[rest], recv_sem.at[1 + final])
         image = state[2, own] * jnp.sum(ends[...], axis=0) + state[3, own]
-        balanced_ref[...] = state[0, own] + state[2, own] * (alpha * state[4, own])
-        residual_ref[...] = state[1, own] - alpha * image
+        out_ref[0] = state[0, own] + state[2, own] * (alpha * state[4, own])
+        out_ref[1] = state[1, own] - alpha * image
     else:
-        balanced_ref[...] = state[0, own]
-        residual_ref[...] = state[1, own]
+        out_ref[0] = state[0, own]
+        out_ref[1] = state[1, own]
 
     take(vectors.at[0, others], send_sem.at[0])
     if paired:
@@ -257,21 +264,22 @@
     chunk = 16 if blocks % 16 == 0 else blocks
     members = blocks // 2 if paired else blocks
     block = (halves, LANES)
-    any_space = pl.BlockSpec(memory_space=pl.ANY)
-    smem = pl.BlockSpec(memory_space=pltpu.SMEM)
+    hbm = pl.BlockSpec(memory_space=pltpu.HBM)
     vmem = pl.BlockSpec(memory_space=pltpu.VMEM)
-    shape = jax.ShapeDtypeStruct((owned,) + block, jnp.float32)
+    shape = jax.ShapeDtypeStruct((2, owned) + block, jnp.float32)
     slots = 1 + 2 * turns
 
     def scratch(*dims):
         return pltpu.VMEM(dims + block, jnp.float32)
 
-    balanced, residual = pl.pallas_call(
+    both = pl.pallas_call(
         functools.partial(kernel, (count, blocks, reps, owned, halves, paired)),
-        out_shape=(shape, shape),
-        in_specs=[any_space, smem, smem, any_space],
-        out_specs=(vmem, vmem),
+        out_shape=shape,
+        in_specs=[hbm] * 4,
+        out_specs=vmem,
         scratch_shapes=[
+            pltpu.SMEM((count,), jnp.int32),
+            pltpu.SMEM((count,), jnp.int32),
             pltpu.VMEM((2 * count, width, width), jnp.float32),
             pltpu.VMEM((chunk, 3 * chunk * halves, width), jnp.bfloat16),
             pltpu.VMEM((blocks, width, LANES), jnp.float32),
@@ -284,6 +292,7 @@
             pltpu.VMEM((members, 1, LANES), jnp.float32),
             pltpu.SemaphoreType.DMA((count,)),
             pltpu.SemaphoreType.DMA,
+            pltpu.SemaphoreType.DMA((2,)),
             pltpu.SemaphoreType.DMA((slots,)),
             pltpu.SemaphoreType.DMA((slots,)),
             pltpu.SemaphoreType.DMA((turns,)),
@@ -294,7 +303,8 @@
         compiler_params=pltpu.CompilerParams(
             collective_id=0, has_side_effects=True, vmem_limit_bytes=56 * 2**20),
     )(tiles, tile_row, tile_col, scaling.reshape((owned,) + block))
-    return balanced.reshape(-1), residual.reshape(-1)
+    both = both.reshape(2, -1)
+    return both[0], both[1]
 
 
 def solution(mesh):

time: 36.4 us -> 33.7 us (0.926)
  Pallas kernels: 33 us -> 31.6 us
  local copies, waits for them, and re-layouts: 2.53 us -> 1.28 us
    unnamed x2 -> x0, local copies, waits for them, and re-layouts: 2.53 us -> none
    pallas_call x1, Pallas kernels: 33 us -> 31.6 us  [shards(): pl.pallas_call(functools.partial(kernel, (count, blocks, reps, owned, hal...]
    slice x0 -> x1, local copies, waits for them, and re-layouts: none -> 1.28 us  [shards(): return (both[0], both[1])]
where the time goes in v3:
time: 33.7 us; the launch traced here: 33.5 us
  Pallas kernels  31.6 us (94%)
  local copies, waits for them, and re-layouts  1.28 us (4%)
  between operations  0.64 us (2%)
    pallas_call x1, Pallas kernels, shards(): pl.pallas_call(functools.partial(kernel, (count, blocks, reps, owned, hal...  31.6 us
    slice x1, local copies, waits for them, and re-layouts, shards(): return (both[0], both[1])  1.28 us

profile of v3, /device:TPU:0, one launch (start us, length us, event | category | flops | bytes accessed | tf_op | source)
XLA Modules:
  0.0 33.5 jit_solution(1487871784523658420)
XLA Ops:
  0.6 31.6 %shard_map.59 = f32[2,4,2,128]{3,2,1,0:T(2,128)} custom-call(f32[16,256,256]{2,1,0:T(8,128)} %tiles_hbm.1, s32[16]{0:T(128)} %row_hbm.1, s32[16]{0:T(128)} %col_hbm.1, f32[4,2,128]{2,1,0:T(2,128)} %bitcast.5), custom_call_target="tpu_custom_call" | custom-call | tf_op jit(solution)/shard_map/pallas_call | solution.py:275
  32.2 1.3 %fusion = (f32[1,4,2,128]{3,2,1,0:T(2,128)}, f32[1,4,2,128]{3,2,1,0:T(2,128)}) fusion(f32[2,4,2,128]{3,2,1,0:T(2,128)} %shard_map.59), kind=kLoop, calls=%fused_computation | loop fusion | bytes 16384 | tf_op jit(solution)/shard_map/slice | solution.py:307

commit v4 on v3

--- a/solution.py
+++ b/solution.py
@@ -25,7 +25,7 @@
 
 def kernel(sizes, tiles_hbm, row_hbm, col_hbm, scaling_ref, out_ref,
            row_ref, col_ref,
-           mats, pick, spread, dense, mate, shares, vectors, state, ends, dots,
+           mats, pick, spread, scale_all, dense, mate, shares, state, ends, dots, terms, parcels, blocked,
            tile_sem, scale_sem, index_sem, send_sem, recv_sem, mate_send, mate_recv, dot_send, dot_recv):
     count, blocks, reps, owned, halves, paired = sizes
     places = blocks // owned
@@ -58,6 +58,15 @@
 
     partner = {"rep": r + 1 - 2 * side}
 
+    def send(source, target_ref, slot, device):
+        pltpu.make_async_remote_copy(
+            src_ref=source, dst_ref=target_ref, send_sem=send_sem.at[slot],
+            recv_sem=recv_sem.at[slot], device_id=device, device_id_type=MESH,
+        ).start()
+
+    def take(ref, semaphore):
+        pltpu.make_async_copy(ref, ref, semaphore).wait()
+
     def tile_copy(k):
         return pltpu.make_async_copy(tiles_hbm.at[k], mats.at[count + k], tile_sem.at[k])
 
@@ -76,8 +85,9 @@
         copy.start()
     for k in range(count):
         tile_copy(k).start()
-    own = pl.ds(q * owned, owned)
-    own_scale = pltpu.make_async_copy(scaling_ref, vectors.at[0, own], scale_sem)
+    held = owned * halves
+    own = pl.ds(pl.multiple_of(q * held, held), held)
+    own_scale = pltpu.make_async_copy(scaling_ref, scale_all.at[own], scale_sem)
     own_scale.start()
 
     half_row = lax.broadcasted_iota(jnp.int32, (chunk * halves, width), 0)
@@ -95,7 +105,7 @@
 
     for ahead in range(places - 1, 0, -1):
         pltpu.make_async_remote_copy(
-            src_ref=vectors.at[0, own], dst_ref=vectors.at[0, own],
+            src_ref=scale_all.at[own], dst_ref=scale_all.at[own],
             send_sem=send_sem.at[0], recv_sem=recv_sem.at[0],
             device_id={"tiles": wrap(q + ahead, places)}, device_id_type=MESH,
         ).start()
@@ -105,9 +115,9 @@
         tile_copy(k).wait()
         mats[k] = mats[count + k].T
 
-    others = pl.ds(0, (places - 1) * owned)
+    others = scale_all.at[pl.ds(0, (places - 1) * held)]
     rest = pl.ds(0, members - 1)
-    pltpu.make_async_copy(vectors.at[0, others], vectors.at[0, others], recv_sem.at[0]).wait()
+    take(others, recv_sem.at[0])
 
     line = lax.broadcasted_iota(jnp.int32, (rows, LANES), 0)
 
@@ -139,118 +149,118 @@
         return lax.fori_loop(0, count, both, jnp.zeros((rows, LANES), jnp.float32), unroll=8)
 
     def with_partner(total, turn):
-        dense[turn] = total.reshape(blocks, halves, LANES)
-        swap = pltpu.make_async_remote_copy(
+        dense[turn] = total
+        pltpu.make_async_remote_copy(
             src_ref=dense.at[turn], dst_ref=mate.at[turn],
             send_sem=mate_send.at[turn], recv_sem=mate_recv.at[turn],
-            device_id=partner, device_id_type=MESH)
-        swap.start()
-        swap.wait()
-        return total + mate[turn].reshape(rows, LANES)
-
-    def send(source, target_ref, slot, device):
-        pltpu.make_async_remote_copy(
-            src_ref=source, dst_ref=target_ref, send_sem=send_sem.at[slot],
-            recv_sem=recv_sem.at[slot], device_id=device, device_id_type=MESH,
-        ).start()
-
-    def take(ref, semaphore):
-        pltpu.make_async_copy(ref, ref, semaphore).wait()
+            device_id=partner, device_id_type=MESH).start()
+        take(mate.at[turn], mate_recv.at[turn])
+        return total + mate[turn]
 
     def summed_pairs(vector, turn):
-        total = with_partner(products(vector), turn)
-        shares[turn, me] = total.reshape(blocks, halves, LANES)
+        shares[turn, me] = with_partner(products(vector), turn)
 
         @for_peers
         def _(place, member, target):
             send(shares.at[turn, me], shares.at[turn, me], 1 + turn, target)
 
         take(shares.at[turn, rest], recv_sem.at[1 + turn])
-        return jnp.sum(shares[turn], axis=0).reshape(rows, LANES)
+        return jnp.sum(shares[turn], axis=0)
 
     def summed_blocks(vector, turn):
-        dense[turn] = products(vector).reshape(blocks, halves, LANES)
-        shares[turn, me] = dense[turn, me]
+        terms[turn] = products(vector).reshape(blocks, halves, LANES)
+        parcels[turn, me] = terms[turn, me]
         slot = 1 + 2 * turn
 
         @for_peers
         def _(place, member, target):
-            send(dense.at[turn, member], shares.at[turn, me], slot, target)
-
-        take(shares.at[turn, rest], recv_sem.at[slot])
-        vectors[1 + turn, me] = jnp.sum(shares[turn], axis=0)
+            send(terms.at[turn, member], parcels.at[turn, me], slot, target)
+
+        take(parcels.at[turn, rest], recv_sem.at[slot])
+        blocked[turn, me] = jnp.sum(parcels[turn], axis=0)
 
         @for_peers
         def _(place, member, target):
-            send(vectors.at[1 + turn, me], vectors.at[1 + turn, me], slot + 1, target)
-
-        take(vectors.at[1 + turn, rest], recv_sem.at[slot + 1])
-        return vectors[1 + turn].reshape(rows, LANES)
+            send(blocked.at[turn, me], blocked.at[turn, me], slot + 1, target)
+
+        take(blocked.at[turn, rest], recv_sem.at[slot + 1])
+        return blocked[turn].reshape(rows, LANES)
 
     apply_map = summed_pairs if paired else summed_blocks
 
     def inner(a, b):
         return jnp.sum(a * b, keepdims=True)
 
-    scaling = vectors[0].reshape(rows, LANES)
+    scaling = scale_all[...]
     load = scaling * apply_map(scaling, 0)
     residual = 1.0 - load
     direction = residual
     update = jnp.zeros_like(load)
     norm_now = inner(residual, residual)
+    along = apply_map(scaling * direction, 1)
+    across = along
     for step in range(ITERS):
-        turn = 1 + step
-        if turn == final:
-            break
-        image = scaling * apply_map(scaling * direction, turn) + load * direction
+        turn = 2 + step
+        last = step + 1 == ITERS
+        image = scaling * along + load * direction
         alpha = norm_now / inner(direction, image)
         update = update + alpha * direction
         residual = residual - alpha * image
-        if step + 1 < ITERS:
-            norm_next = inner(residual, residual)
-            direction = residual + (norm_next / norm_now) * direction
-            norm_now = norm_next
-
-    kept = [scaling * (1.0 + update), residual]
-    if paired:
-        kept += [scaling, load * direction, direction]
-    for i, value in enumerate(kept):
-        state[i] = value.reshape(blocks, halves, LANES)
+        if last:
+            break
+        norm_next = inner(residual, residual)
+        ratio = norm_next / norm_now
+        direction = residual + ratio * direction
+        norm_now = norm_next
+        if turn == final:
+            break
+        across = across - alpha * apply_map(scaling * image, turn)
+        along = across + ratio * along
+
     if paired:
         scaled = scaling * direction
-        known = inner(load * direction, direction)
-        total = with_partner(products(scaled), final)
-        dense[1 + final] = total.reshape(blocks, halves, LANES)
+        before = across + ratio * along
+        known = inner(scaled, before) + inner(load * direction, direction)
+        kept = (scaling * (1.0 + update), residual, scaling, scaling * before + load * direction, direction)
+        for i, value in enumerate(kept):
+            state[i] = value
+        total = with_partner(products(scaling * image), final)
+        dense[1 + final] = total
         ends[me] = dense[1 + final, own]
         dots[me] = jnp.broadcast_to(inner(scaled, total), (1, LANES))
 
         @for_peers
         def _(place, member, target):
-            send(dense.at[1 + final, pl.ds(place * owned, owned)], ends.at[me], 1 + final, target)
+            part = pl.ds(pl.multiple_of(place * held, held), held)
+            send(dense.at[1 + final, part], ends.at[me], 1 + final, target)
             pltpu.make_async_remote_copy(
                 src_ref=dots.at[me], dst_ref=dots.at[me], send_sem=dot_send,
                 recv_sem=dot_recv, device_id=target, device_id_type=MESH,
             ).start()
 
         take(dots.at[rest], dot_recv)
-        alpha = norm_now / (known + jnp.sum(dots[...], axis=0)[:, :1])
+        step_size = norm_now / (known - alpha * jnp.sum(dots[...], axis=0)[:, :1])
         take(ends.at[rest], recv_sem.at[1 + final])
-        image = state[2, own] * jnp.sum(ends[...], axis=0) + state[3, own]
-        out_ref[0] = state[0, own] + state[2, own] * (alpha * state[4, own])
-        out_ref[1] = state[1, own] - alpha * image
+        image = state[3, own] - alpha * (state[2, own] * jnp.sum(ends[...], axis=0))
+        out_ref[0] = state[0, own] + state[2, own] * (step_size * state[4, own])
+        out_ref[1] = state[1, own] - step_size * image
     else:
+        state[0] = scaling * (1.0 + update)
+        state[1] = residual
         out_ref[0] = state[0, own]
         out_ref[1] = state[1, own]
 
-    take(vectors.at[0, others], send_sem.at[0])
+    take(others, send_sem.at[0])
     if paired:
         for turn in range(final):
             take(shares.at[turn, rest], send_sem.at[1 + turn])
+        for turn in range(1 + final):
+            take(mate.at[turn], mate_send.at[turn])
         take(ends.at[rest], send_sem.at[1 + final])
         take(dots.at[rest], dot_send)
     else:
         for slot in range(1, 3 + 2 * ITERS):
-            take(shares.at[0, rest], send_sem.at[slot])
+            take(blocked.at[0, rest], send_sem.at[slot])
 
 
 def shards(places, reps, tiles, tile_row, tile_col, scaling):
@@ -263,18 +273,18 @@
     paired = reps % 2 == 0 and places * reps <= 32
     chunk = 16 if blocks % 16 == 0 else blocks
     members = blocks // 2 if paired else blocks
-    block = (halves, LANES)
+    rows, held = blocks * halves, owned * halves
     hbm = pl.BlockSpec(memory_space=pltpu.HBM)
     vmem = pl.BlockSpec(memory_space=pltpu.VMEM)
-    shape = jax.ShapeDtypeStruct((2, owned) + block, jnp.float32)
     slots = 1 + 2 * turns
 
     def scratch(*dims):
-        return pltpu.VMEM(dims + block, jnp.float32)
-
+        return pltpu.VMEM(dims + (LANES,), jnp.float32)
+
+    some, none = (turns, 1) if paired else (1, turns)
     both = pl.pallas_call(
         functools.partial(kernel, (count, blocks, reps, owned, halves, paired)),
-        out_shape=shape,
+        out_shape=pltpu.VMEM((2, held, LANES), jnp.float32),
         in_specs=[hbm] * 4,
         out_specs=vmem,
         scratch_shapes=[
@@ -283,13 +293,16 @@
             pltpu.VMEM((2 * count, width, width), jnp.float32),
             pltpu.VMEM((chunk, 3 * chunk * halves, width), jnp.bfloat16),
             pltpu.VMEM((blocks, width, LANES), jnp.float32),
-            scratch(turns + 1, blocks),
-            scratch(turns, blocks),
-            scratch(turns, members, blocks) if paired else scratch(turns, members),
-            scratch(1 + turns, blocks),
-            scratch(5, blocks),
-            scratch(members, owned),
-            pltpu.VMEM((members, 1, LANES), jnp.float32),
+            scratch(rows),
+            scratch(some + 1, rows),
+            scratch(some, rows),
+            scratch(some, members if paired else 1, rows),
+            scratch(5, rows),
+            scratch(members, held),
+            scratch(members, 1),
+            scratch(none, blocks, halves),
+            scratch(none, members, halves),
+            scratch(none, blocks, halves),
             pltpu.SemaphoreType.DMA((count,)),
             pltpu.SemaphoreType.DMA,
             pltpu.SemaphoreType.DMA((2,)),
@@ -302,7 +315,7 @@
         ],
         compiler_params=pltpu.CompilerParams(
             collective_id=0, has_side_effects=True, vmem_limit_bytes=56 * 2**20),
-    )(tiles, tile_row, tile_col, scaling.reshape((owned,) + block))
+    )(tiles, tile_row, tile_col, scaling.reshape(held, LANES))
     both = both.reshape(2, -1)
     return both[0], both[1]
 

time: 33.7 us -> 30.2 us (0.90)
  Pallas kernels: 31.6 us -> 28.8 us
  local copies, waits for them, and re-layouts: 1.28 us -> 0.6 us
    pallas_call x1, Pallas kernels: 31.6 us -> 28.8 us  [shards(): pl.pallas_call(functools.partial(kernel, (count, blocks, reps, owned, hal...]
    slice x1 -> x0, local copies, waits for them, and re-layouts: 1.28 us -> none  [shards(): return (both[0], both[1])]
    squeeze x0 -> x1, local copies, waits for them, and re-layouts: none -> 0.6 us  [shards(): return (both[0], both[1])]
where the time goes in v4:
time: 30.2 us; the launch traced here: 30.1 us
  Pallas kernels  28.8 us (95%)
  between operations  0.64 us (2%)
  local copies, waits for them, and re-layouts  0.6 us (2%)
    pallas_call x1, Pallas kernels, shards(): pl.pallas_call(functools.partial(kernel, (count, blocks, reps, owned, hal...  28.8 us

profile of v4, /device:TPU:0, one launch (start us, length us, event | category | flops | bytes accessed | tf_op | source)
XLA Modules:
  0.0 30.1 jit_solution(13171991562520583557)
XLA Ops:
  0.6 28.8 %shard_map.59 = f32[2,8,128]{2,1,0:T(8,128)S(1)} custom-call(f32[16,256,256]{2,1,0:T(8,128)} %tiles_hbm.1, s32[16]{0:T(128)} %row_hbm.1, s32[16]{0:T(128)} %col_hbm.1, f32[8,128]{1,0:T(8,128)} %bitcast.5), custom_call_target="tpu_custom_call" | custom-call | tf_op jit(solution)/shard_map/pallas_call | solution.py:285
  29.5 0.6 %slice_bitcast_fusion = (f32[1024]{0:T(1024)}, f32[1024]{0:T(1024)}) fusion(f32[2,8,128]{2,1,0:T(8,128)S(1)} %shard_map.59), kind=kLoop, calls=%fused_computation | loop fusion | bytes 16384 | tf_op jit(solution)/shard_map/squeeze | solution.py:320

commit v5 on v4

--- a/solution.py
+++ b/solution.py
@@ -45,7 +45,7 @@
     def for_peers(act):
         def column(ahead, first):
             place = wrap(q + ahead, places)
-            for turn in range(first, turn_reps):
+            for turn in reversed(range(first, turn_reps)):
                 member = wrap(mine + turn, turn_reps)
                 act(place, place * turn_reps + member, {"tiles": place, "rep": member * lanes + side})
 

time: 30.2 us -> 29.9 us (0.990)
    pallas_call x1, Pallas kernels: 28.8 us -> 28.5 us  [shards(): pl.pallas_call(functools.partial(kernel, (count, blocks, reps, owned, hal...]
where the time goes in v5:
time: 29.9 us; the launch traced here: 29.8 us
  Pallas kernels  28.5 us (95%)
  between operations  0.64 us (2%)
  local copies, waits for them, and re-layouts  0.6 us (2%)
    pallas_call x1, Pallas kernels, shards(): pl.pallas_call(functools.partial(kernel, (count, blocks, reps, owned, hal...  28.5 us
    squeeze x1, local copies, waits for them, and re-layouts, shards(): return (both[0], both[1])  0.6 us

profile of v5, /device:TPU:0, one launch (start us, length us, event | category | flops | bytes accessed | tf_op | source)
XLA Modules:
  0.0 29.8 jit_solution(12009060237760694045)
XLA Ops:
  0.6 28.5 %shard_map.59 = f32[2,8,128]{2,1,0:T(8,128)S(1)} custom-call(f32[16,256,256]{2,1,0:T(8,128)} %tiles_hbm.1, s32[16]{0:T(128)} %row_hbm.1, s32[16]{0:T(128)} %col_hbm.1, f32[8,128]{1,0:T(8,128)} %bitcast.5), custom_call_target="tpu_custom_call" | custom-call | tf_op jit(solution)/shard_map/pallas_call | solution.py:285
  29.2 0.6 %slice_bitcast_fusion = (f32[1024]{0:T(1024)}, f32[1024]{0:T(1024)}) fusion(f32[2,8,128]{2,1,0:T(8,128)S(1)} %shard_map.59), kind=kLoop, calls=%fused_computation | loop fusion | bytes 16384 | tf_op jit(solution)/shard_map/squeeze | solution.py:320
